TPU v7x, 1024 devices: a whole 4x4x32 slice. The times are simulated.
1024 devices in a mesh: row: 32 (over z_lo, core), col: 32 (over y, x, z_hi).
Axes of the slice: x: 4, y: 4, z: 32 (z_hi: 2, z_lo: 16; z = z_hi * 16 + z_lo), core: 2. Of those that a mesh axis runs over, the one named last changes fastest.
Arguments:
- a_tiles: bfloat16 [32, 640, 128, 128], P('row', 'col'), may hold values from -6 to 6
- a_where: int32 [32, 640], P('row', 'col'), may hold values from 0 to 63, as said below
- a_count: int32 [32, 32], P('row', 'col'), may hold values from 6 to 20, as said below
- b_tiles: bfloat16 [32, 960, 128, 128], P('row', 'col'), may hold values from -0.125 to 0.125
- b_where: int32 [32, 960], P('row', 'col'), may hold values from 0 to 95, as said below
- b_count: int32 [32, 32], P('row', 'col'), may hold values from 10 to 30, as said below
Outputs:
- c_slab: bfloat16 [16384, 24576], P('row', 'col')
Inputs may be any that keep to these rules, and one draw needn't show every extreme that they name: `a_where`: within one device the positions of its 20 slots are distinct. `a_count`: some device has all 20 slots occupied in every draw. `b_where`: within one device the positions of its 30 slots are distinct. `b_count`: some device has all 30 slots occupied in every draw.
All inputs are finite; a program needn't handle non-finite values.
Results may differ from a plain program's by a relative error of at most 0.001.
Values may be sent and summed in bfloat16 or wider, within the bound.
No kernel may reach another device: no remote copies, remote signals or barrier semaphores. Data moves between devices by JAX's collectives and lax.ppermute only.
A program may use at most 32 MiB of HBM per device.

v0:
```python
import jax
import jax.numpy as jnp
from jax import lax
from jax.sharding import PartitionSpec as P

MT = 4
KT = 16
NT = 6


def passed_along(array, axis, by):
    size = lax.axis_size(axis)
    return lax.ppermute(array, axis, [(i, (i + by) % size) for i in range(size)])


def positions(where, count, rows, cols):
    live = jnp.arange(where.shape[1])[None, :] < count
    return jnp.where(live, where, rows * cols)[0]


def unpack(tiles, spots, rows, cols):
    edge = tiles.shape[-1]
    dense = (
        jnp.zeros((rows * cols + 1, edge, edge), tiles.dtype).at[spots].set(tiles)[: rows * cols]
    )
    return (
        dense.reshape(rows, cols, edge, edge)
        .transpose(0, 2, 1, 3)
        .reshape(rows * edge, cols * edge)
    )


def shards(a_tiles, a_where, a_count, b_tiles, b_where, b_count):
    left_spots = positions(a_where, a_count, MT, KT)
    right_spots = positions(b_where, b_count, KT, NT)
    left_here = unpack(a_tiles[0], left_spots, MT, KT)
    right_here = unpack(b_tiles[0], right_spots, KT, NT)
    left_next = passed_along(left_here, "col", -1)
    right_next = passed_along(right_here, "row", -1)
    total = jnp.dot(left_here, right_here, preferred_element_type=jnp.float32)
    total = total + jnp.dot(left_next, right_next, preferred_element_type=jnp.float32)
    return total.astype(jnp.bfloat16)


def solution(mesh):
    in_specs = (
        P("row", "col", None, None),
        P("row", "col"),
        P("row", "col"),
        P("row", "col", None, None),
        P("row", "col"),
        P("row", "col"),
    )
    out_specs = P("row", "col")
    return jax.shard_map(shards, mesh=mesh, in_specs=in_specs, out_specs=out_specs, check_vma=False)
```

profile of v0, /device:TPU:979, one launch (start us, length us, event | category | flops | bytes accessed | tf_op | source)
XLA Modules:
  0.0 444.2 jit_solution(4917863464623091926)
XLA Ops:
  0.7 0.7 fusion.2
  1.3 0.8 broadcast_in_dim.20
  2.1 3.6 scatter_fusion.1
  5.7 1.9 slice.9
  7.6 3.8 copy.8
  11.4 0.0 copy-start
  11.4 3.0 copy.15
  14.4 2.6 collective-permute-start.1
  17.6 0.0 copy-done
  17.6 1.9 broadcast_in_dim.18
  19.5 5.5 %scatter_fusion = bf16[65,128,128]{2,1,0:T(8,128)(2,1)} fusion(bf16[65,128,128]{2,1,0:T(8,128)(2,1)} %broadcast_in_dim.18, s32[20]{0:T(128)S(1)} %fusion.3, bf16[20,128,128]{2,1,0:T(8,128)(2,1)} %bitcast.52), kind=kCustom, calls=%fused_computation | custom fusion | bytes 1966160 | tf_op jit(solution)/shard_map/scatter | solution.py:24
  25.0 1.7 slice.8
  26.7 1.4 copy.7
  28.1 0.5 copy.16
  28.6 11.1 %collective-permute-start = (bf16[512,2048]{1,0:T(8,128)(2,1)S(1)}, bf16[512,2048]{1,0:T(8,128)(2,1)S(1)}, u32[]{:S(2)}, u32[]{:S(2)}) collective-permute-start(bf16[512,2048]{1,0:T(8,128)(2,1)S(1)} %bitcast.50), channel_id=1, source_target_pairs={{0,31},{1,0},{2,1},{3,2},{4,3},{5,4},{6,5},{7,6},{8,7},{9,8},{10,9... | collective-permute-start | bytes 6291464 | tf_op jit(solution)/shard_map/ppermute | solution.py:13
  39.8 1.8 fusion.4
  41.6 397.9 %collective-permute-done = bf16[512,2048]{1,0:T(8,128)(2,1)S(1)} collective-permute-done((bf16[512,2048]{1,0:T(8,128)(2,1)S(1)}, bf16[512,2048]{1,0:T(8,128)(2,1)S(1)}, u32[]{:S(2)}, u32[]{:S(2)}) %collective-permute-start) | collective-permute-done | bytes 2097184 | tf_op jit(solution)/shard_map/ppermute | solution.py:13
  439.5 0.0 collective-permute-done.1
  439.5 4.7 %add_convert_fusion = bf16[512,768]{1,0:T(8,128)(2,1)} fusion(f32[512,768]{1,0:T(8,128)S(1)} %fusion.4, bf16[512,2048]{1,0:T(8,128)(2,1)S(1)} %collective-permute-done, bf16[2048,768]{0,1:T(8,128)(2,1)} %collective-permute-done.1), kind=kOutput, calls=%fused_computation.4 | convolution fusion | flops 1611399168 | bytes 7602176 | tf_op jit(solution)/shard_map/dot_general | solution.py:41
  (1 shorter events, 0.0 us)
Async XLA Ops:
  11.4 6.2 %copy-start = (s32[1,20]{1,0:T(1,128)S(1)}, s32[1,20]{1,0:T(1,128)}, u32[]{:S(2)}) copy-start(s32[1,20]{1,0:T(1,128)} %param.7) | copy-start | bytes 244
  14.4 425.1 %collective-permute-start.1 = (bf16[2048,768]{0,1:T(8,128)(2,1)}, bf16[2048,768]{0,1:T(8,128)(2,1)}, u32[]{:S(2)}, u32[]{:S(2)}) collective-permute-start(bf16[2048,768]{0,1:T(8,128)(2,1)} %bitcast.40), channel_id=1, source_target_pairs={{0,992},{32,0},{64,32},{96,64},{128,96},{160,128},{192,160},{224,1... | collective-permute-start | bytes 9437192 | tf_op jit(solution)/shard_map/ppermute | solution.py:13
  28.6 410.8 %collective-permute-start = (bf16[512,2048]{1,0:T(8,128)(2,1)S(1)}, bf16[512,2048]{1,0:T(8,128)(2,1)S(1)}, u32[]{:S(2)}, u32[]{:S(2)}) collective-permute-start(bf16[512,2048]{1,0:T(8,128)(2,1)S(1)} %bitcast.50), channel_id=1, source_target_pairs={{0,31},{1,0},{2,1},{3,2},{4,3},{5,4},{6,5},{7,6},{8,7},{9,8},{10,9... | collective-permute-start | bytes 6291464 | tf_op jit(solution)/shard_map/ppermute | solution.py:13
where the time goes:
time: 445 us; the launch traced here: 444 us
  waiting for transfers between devices  398 us (89%)
  local copies, waits for them, and re-layouts  24 us (5%)
  starting transfers between devices  13.7 us (3%)
  matrix products  6.53 us (1%)
    ppermute x2, waiting for transfers between devices, passed_along(): lax.ppermute(array, axis, [(i, (i + by) % size) for i in range(size)])  398 us
    ppermute x2, starting transfers between devices, passed_along(): lax.ppermute(array, axis, [(i, (i + by) % size) for i in range(size)])  13.7 us
    scatter x2, local copies, waits for them, and re-layouts, unpack(): jnp.zeros((rows * cols + 1, edge, edge), tiles.dtype).at[spots].set(tiles)  9.05 us
  transfers between devices with their start and end apart: 2, of which 1 were waited for; matrix products, arithmetic and copies ran while one was open for 3% of the time, Pallas kernels for 0%

commit v1 on v0

v1 whole, which is shorter than its diff:
```python
import jax
import jax.numpy as jnp
from jax import lax
from jax.experimental import pallas as pl
from jax.experimental.pallas import tpu as pltpu
from jax.sharding import PartitionSpec as P

TILE = 128
MT = 4
KT = 16
NT = 6
STRIP = 256
VMEM_LIMIT = 40 * 1024 * 1024


def passed_along(array, axis, by):
    size = lax.axis_size(axis)
    return lax.ppermute(array, axis, [(i, (i + by) % size) for i in range(size)])


def place(tiles, spots, count, dense, cols):
    dense[...] = jnp.zeros_like(dense)

    @pl.loop(0, count)
    def _(slot):
        spot = spots[0, slot]
        row = pl.multiple_of((spot // cols) * TILE, TILE)
        col = pl.multiple_of((spot % cols) * TILE, TILE)
        dense[pl.ds(row, TILE), pl.ds(col, TILE)] = tiles[slot]


def first_kernel(a_spots, a_count, b_spots, b_count, a_tiles, b_tiles, total, a_meta, b_meta, left, right):
    for spots, count, meta in ((a_spots, a_count, a_meta), (b_spots, b_count, b_meta)):
        slots = spots.shape[1]

        @pl.loop(0, slots)
        def _(slot):
            meta[0, slot] = spots[0, slot]

        meta[0, slots] = count[0, 0]
    place(a_tiles, a_spots, a_count[0, 0], left, KT)
    place(b_tiles, b_spots, b_count[0, 0], right, NT)
    for strip in range(0, NT * TILE, STRIP):
        cols = pl.ds(strip, STRIP)
        total[:, cols] = jnp.dot(left[...], right[:, cols], preferred_element_type=jnp.float32)


def place_kernel(b_meta, b_tiles, right):
    place(b_tiles, b_meta, b_meta[0, b_tiles.shape[0]], right, NT)


def last_kernel(a_meta, a_tiles, right, total, out, left):
    @pl.when(pl.program_id(0) == 0)
    def _():
        place(a_tiles, a_meta, a_meta[0, a_tiles.shape[0]], left, KT)

    added = jnp.dot(left[...], right[...], preferred_element_type=jnp.float32)
    out[...] = (total[...] + added).astype(out.dtype)


def shards(a_tiles, a_where, a_count, b_tiles, b_where, b_count):
    a_tiles, b_tiles = a_tiles[0], b_tiles[0]
    slots_a, slots_b = a_tiles.shape[0], b_tiles.shape[0]
    rows, depth, cols = MT * TILE, KT * TILE, NT * TILE
    smem = pl.BlockSpec(memory_space=pltpu.SMEM)
    vmem = pl.BlockSpec(memory_space=pltpu.VMEM)
    params = pltpu.CompilerParams(vmem_limit_bytes=VMEM_LIMIT)
    macs = rows * depth * cols

    b_next = passed_along(b_tiles, "row", -1)
    a_next = passed_along(a_tiles, "col", -1)

    total, a_meta, b_meta = pl.pallas_call(
        first_kernel,
        out_shape=(
            jax.ShapeDtypeStruct((rows, cols), jnp.float32),
            jax.ShapeDtypeStruct((1, slots_a + 1), jnp.int32),
            jax.ShapeDtypeStruct((1, slots_b + 1), jnp.int32),
        ),
        in_specs=[smem, smem, smem, smem, vmem, vmem],
        out_specs=(vmem, smem, smem),
        scratch_shapes=[
            pltpu.VMEM((rows, depth), jnp.bfloat16),
            pltpu.VMEM((depth, cols), jnp.bfloat16),
        ],
        compiler_params=params,
        cost_estimate=pl.CostEstimate(flops=2 * macs, bytes_accessed=8 << 20, transcendentals=0),
    )(a_where, a_count, b_where, b_count, a_tiles, b_tiles)

    a_meta = passed_along(a_meta, "col", -1)
    b_meta = passed_along(b_meta, "row", -1)

    right = pl.pallas_call(
        place_kernel,
        out_shape=jax.ShapeDtypeStruct((depth, cols), jnp.bfloat16),
        in_specs=[smem, vmem],
        out_specs=vmem,
        compiler_params=params,
        cost_estimate=pl.CostEstimate(flops=0, bytes_accessed=8 << 20, transcendentals=0),
    )(b_meta, b_next)

    return pl.pallas_call(
        last_kernel,
        grid=(cols // STRIP,),
        out_shape=jax.ShapeDtypeStruct((rows, cols), jnp.bfloat16),
        in_specs=[
            smem,
            pl.BlockSpec((slots_a, TILE, TILE), lambda n: (0, 0, 0)),
            pl.BlockSpec((depth, STRIP), lambda n: (0, n)),
            pl.BlockSpec((rows, STRIP), lambda n: (0, n)),
        ],
        out_specs=pl.BlockSpec((rows, STRIP), lambda n: (0, n)),
        scratch_shapes=[pltpu.VMEM((rows, depth), jnp.bfloat16)],
        compiler_params=params,
        cost_estimate=pl.CostEstimate(flops=2 * macs, bytes_accessed=8 << 20, transcendentals=0),
    )(a_meta, a_next, right, total)


def solution(mesh):
    in_specs = (
        P("row", "col", None, None),
        P("row", "col"),
        P("row", "col"),
        P("row", "col", None, None),
        P("row", "col"),
        P("row", "col"),
    )
    out_specs = P("row", "col")
    return jax.shard_map(shards, mesh=mesh, in_specs=in_specs, out_specs=out_specs, check_vma=False)
```

time: 445 us -> 158 us (0.36)
  the two profiles are of different devices: /device:TPU:979 before, /device:TPU:64 now
where the time goes in v1:
time: 158 us
  waiting for transfers between devices  106 us (67%)
  starting transfers between devices  38.4 us (24%)
  Pallas kernels  8.95 us (6%)
  local copies, waits for them, and re-layouts  3.59 us (2%)
    ppermute x4, waiting for transfers between devices, passed_along(): lax.ppermute(array, axis, [(i, (i + by) % size) for i in range(size)])  106 us
    ppermute x4, starting transfers between devices, passed_along(): lax.ppermute(array, axis, [(i, (i + by) % size) for i in range(size)])  38.4 us
    pallas_call x1, Pallas kernels, shards(): pl.pallas_call(last_kernel, grid=(cols // STRIP,), out_shape=jax.ShapeDty...  4.06 us
    pallas_call x1, Pallas kernels, shards(): pl.pallas_call(first_kernel, out_shape=(jax.ShapeDtypeStruct((rows, cols)...  3.75 us
    unnamed x8, local copies, waits for them, and re-layouts  3.59 us
  transfers between devices with their start and end apart: 4, of which 1 were waited for; matrix products, arithmetic and copies ran while one was open for 0% of the time, Pallas kernels for 3%

profile of v1, /device:TPU:64, one launch (start us, length us, event | category | flops | bytes accessed | tf_op | source)
XLA Modules:
  0.0 157.8 jit_solution(2845121382591487156)
XLA Ops:
  0.0 1.9 %collective-permute-start.3 = (bf16[30,128,128]{2,1,0:T(8,128)(2,1)}, bf16[30,128,128]{2,1,0:T(8,128)(2,1)S(1)}, u32[]{:S(2)}, u32[]{:S(2)}) collective-permute-start(bf16[30,128,128]{2,1,0:T(8,128)(2,1)} %bitcast.2), channel_id=1, source_target_pairs={{0,992},{32,0},{64,32},{96,64},{128,96},{160,128},{192,160},{224,1... | collective-permute-start | bytes 2949128 | tf_op jit(solution)/shard_map/ppermute | solution.py:18
  1.9 32.3 %collective-permute-start.1 = (bf16[20,128,128]{2,1,0:T(8,128)(2,1)}, bf16[20,128,128]{2,1,0:T(8,128)(2,1)S(1)}, u32[]{:S(2)}, u32[]{:S(2)}) collective-permute-start(bf16[20,128,128]{2,1,0:T(8,128)(2,1)} %bitcast.4), channel_id=1, source_target_pairs={{0,31},{1,0},{2,1},{3,2},{4,3},{5,4},{6,5},{7,6},{8,7},{9,8},{10,9... | collective-permute-start | bytes 1966088 | tf_op jit(solution)/shard_map/ppermute | solution.py:18
  35.5 0.0 copy-start
  35.5 1.2 copy-done
  36.7 0.0 copy-start.1
  36.7 1.1 copy-done.1
  37.8 0.0 copy-start.2
  37.8 0.7 copy-done.2
  38.4 0.0 copy-start.3
  38.4 0.7 copy-done.3
  39.1 3.8 %shard_map.64 = (f32[512,768]{1,0:T(8,128)S(1)}, s32[1,21]{1,0:T(1,128)S(1)}, s32[1,31]{1,0:T(1,128)S(1)}) custom-call(s32[1,20]{1,0:T(1,128)S(1)} %copy-done.2, s32[1,1]{1,0:T(1,128)S(6)} %copy.7.a_count, s32[1,30]{1,0:T(1,128)S(1)} %copy-done.3, s32[1,1]{1,0:T(1,128)S(6)} %copy.8.b_count, bf16[20,128,128]{2,1,0:T(8,128)(2,1)S(1)} %bitcast.5, ...), custom_call_target="tpu_custom_call" | custom-call | flops 1610612736 | bytes 8388608 | tf_op jit(solution)/shard_map/pallas_call | solution.py:73
  42.8 2.2 %collective-permute-start.2 = (s32[1,31]{1,0:T(1,128)S(1)}, s32[1,31]{1,0:T(1,128)S(1)}, u32[]{:S(2)}, u32[]{:S(2)}) collective-permute-start(s32[1,31]{1,0:T(1,128)S(1)} %get-tuple-element.9), channel_id=1, source_target_pairs={{0,992},{32,0},{64,32},{96,64},{128,96},{160,128},{192,160},{224,1... | collective-permute-start | bytes 380 | tf_op jit(solution)/shard_map/ppermute | solution.py:18
  45.1 2.0 %collective-permute-start = (s32[1,21]{1,0:T(1,128)S(1)}, s32[1,21]{1,0:T(1,128)S(1)}, u32[]{:S(2)}, u32[]{:S(2)}) collective-permute-start(s32[1,21]{1,0:T(1,128)S(1)} %get-tuple-element.8), channel_id=1, source_target_pairs={{0,31},{1,0},{2,1},{3,2},{4,3},{5,4},{6,5},{7,6},{8,7},{9,8},{10,9... | collective-permute-start | bytes 260 | tf_op jit(solution)/shard_map/ppermute | solution.py:18
  47.1 0.0 collective-permute-done.2.b_meta
  47.1 0.0 collective-permute-done.3.b_tiles
  47.1 1.1 shard_map.65.right
  48.2 105.5 %collective-permute-done.a_meta = s32[1,21]{1,0:T(1,128)S(1)} collective-permute-done((s32[1,21]{1,0:T(1,128)S(1)}, s32[1,21]{1,0:T(1,128)S(1)}, u32[]{:S(2)}, u32[]{:S(2)}) %collective-permute-start) | collective-permute-done | bytes 116 | tf_op jit(solution)/shard_map/ppermute | solution.py:18
  153.7 0.0 collective-permute-done.1.a_tiles
  153.7 4.1 %shard_map.66 = bf16[512,768]{1,0:T(8,128)(2,1)} custom-call(s32[1,21]{1,0:T(1,128)S(1)} %collective-permute-done.a_meta, bf16[20,128,128]{2,1,0:T(8,128)(2,1)S(1)} %collective-permute-done.1.a_tiles, bf16[2048,768]{1,0:T(8,128)(2,1)S(1)} %shard_map.65.right, f32[512,768]{1,0:T(8,128)S(1)} %get-tuple-element.10.total), custom_call_target="tpu_custom_call" | custom-call | flops 1610612736 | bytes 8388608 | tf_op jit(solution)/shard_map/pallas_call | solution.py:102
Async XLA Ops:
  0.0 47.1 %collective-permute-start.3 = (bf16[30,128,128]{2,1,0:T(8,128)(2,1)}, bf16[30,128,128]{2,1,0:T(8,128)(2,1)S(1)}, u32[]{:S(2)}, u32[]{:S(2)}) collective-permute-start(bf16[30,128,128]{2,1,0:T(8,128)(2,1)} %bitcast.2), channel_id=1, source_target_pairs={{0,992},{32,0},{64,32},{96,64},{128,96},{160,128},{192,160},{224,1... | collective-permute-start | bytes 2949128 | tf_op jit(solution)/shard_map/ppermute | solution.py:18
  1.9 151.8 %collective-permute-start.1 = (bf16[20,128,128]{2,1,0:T(8,128)(2,1)}, bf16[20,128,128]{2,1,0:T(8,128)(2,1)S(1)}, u32[]{:S(2)}, u32[]{:S(2)}) collective-permute-start(bf16[20,128,128]{2,1,0:T(8,128)(2,1)} %bitcast.4), channel_id=1, source_target_pairs={{0,31},{1,0},{2,1},{3,2},{4,3},{5,4},{6,5},{7,6},{8,7},{9,8},{10,9... | collective-permute-start | bytes 1966088 | tf_op jit(solution)/shard_map/ppermute | solution.py:18
  35.5 1.2 copy-start
  36.7 1.1 copy-start.1
  37.8 0.7 copy-start.2
  38.4 0.7 copy-start.3
  42.8 4.2 %collective-permute-start.2 = (s32[1,31]{1,0:T(1,128)S(1)}, s32[1,31]{1,0:T(1,128)S(1)}, u32[]{:S(2)}, u32[]{:S(2)}) collective-permute-start(s32[1,31]{1,0:T(1,128)S(1)} %get-tuple-element.9), channel_id=1, source_target_pairs={{0,992},{32,0},{64,32},{96,64},{128,96},{160,128},{192,160},{224,1... | collective-permute-start | bytes 380 | tf_op jit(solution)/shard_map/ppermute | solution.py:18
  45.1 108.7 %collective-permute-start = (s32[1,21]{1,0:T(1,128)S(1)}, s32[1,21]{1,0:T(1,128)S(1)}, u32[]{:S(2)}, u32[]{:S(2)}) collective-permute-start(s32[1,21]{1,0:T(1,128)S(1)} %get-tuple-element.8), channel_id=1, source_target_pairs={{0,31},{1,0},{2,1},{3,2},{4,3},{5,4},{6,5},{7,6},{8,7},{9,8},{10,9... | collective-permute-start | bytes 260 | tf_op jit(solution)/shard_map/ppermute | solution.py:18

commit v2 on v1

--- a/solution.py
+++ b/solution.py
@@ -10,7 +10,7 @@
 KT = 16
 NT = 6
 STRIP = 256
-VMEM_LIMIT = 40 * 1024 * 1024
+VMEM_LIMIT = 24 * 1024 * 1024
 
 
 def passed_along(array, axis, by):
@@ -50,12 +50,11 @@
 
 
 def last_kernel(a_meta, a_tiles, right, total, out, left):
-    @pl.when(pl.program_id(0) == 0)
-    def _():
-        place(a_tiles, a_meta, a_meta[0, a_tiles.shape[0]], left, KT)
-
-    added = jnp.dot(left[...], right[...], preferred_element_type=jnp.float32)
-    out[...] = (total[...] + added).astype(out.dtype)
+    place(a_tiles, a_meta, a_meta[0, a_tiles.shape[0]], left, KT)
+    for strip in range(0, NT * TILE, STRIP):
+        cols = pl.ds(strip, STRIP)
+        added = jnp.dot(left[...], right[:, cols], preferred_element_type=jnp.float32)
+        out[:, cols] = (total[:, cols] + added).astype(out.dtype)
 
 
 def shards(a_tiles, a_where, a_count, b_tiles, b_where, b_count):
@@ -101,15 +100,9 @@
 
     return pl.pallas_call(
         last_kernel,
-        grid=(cols // STRIP,),
         out_shape=jax.ShapeDtypeStruct((rows, cols), jnp.bfloat16),
-        in_specs=[
-            smem,
-            pl.BlockSpec((slots_a, TILE, TILE), lambda n: (0, 0, 0)),
-            pl.BlockSpec((depth, STRIP), lambda n: (0, n)),
-            pl.BlockSpec((rows, STRIP), lambda n: (0, n)),
-        ],
-        out_specs=pl.BlockSpec((rows, STRIP), lambda n: (0, n)),
+        in_specs=[smem, vmem, vmem, vmem],
+        out_specs=vmem,
         scratch_shapes=[pltpu.VMEM((rows, depth), jnp.bfloat16)],
         compiler_params=params,
         cost_estimate=pl.CostEstimate(flops=2 * macs, bytes_accessed=8 << 20, transcendentals=0),

time: 158 us -> 158 us (level)
  no operation moved by 1% of the time
where the time goes in v2:
time: 158 us; the launch traced here: 157 us
  waiting for transfers between devices  105 us (66%)
  starting transfers between devices  38.9 us (25%)
  Pallas kernels  8.57 us (5%)
  local copies, waits for them, and re-layouts  3.59 us (2%)
    ppermute x4, waiting for transfers between devices, passed_along(): lax.ppermute(array, axis, [(i, (i + by) % size) for i in range(size)])  105 us
    ppermute x4, starting transfers between devices, passed_along(): lax.ppermute(array, axis, [(i, (i + by) % size) for i in range(size)])  38.9 us
    pallas_call x1, Pallas kernels, shards(): pl.pallas_call(last_kernel, out_shape=jax.ShapeDtypeStruct((rows, cols),...  3.69 us
    unnamed x8, local copies, waits for them, and re-layouts  3.59 us
    pallas_call x1, Pallas kernels, shards(): pl.pallas_call(first_kernel, out_shape=(jax.ShapeDtypeStruct((rows, cols)...  3.58 us
  transfers between devices with their start and end apart: 4, of which 1 were waited for; matrix products, arithmetic and copies ran while one was open for 0% of the time, Pallas kernels for 3%

profile of v2, /device:TPU:64, one launch (start us, length us, event | category | flops | bytes accessed | tf_op | source)
XLA Modules:
  0.0 157.4 jit_solution(3429155604404685630)
XLA Ops:
  0.0 1.9 %collective-permute-start.3 = (bf16[30,128,128]{2,1,0:T(8,128)(2,1)}, bf16[30,128,128]{2,1,0:T(8,128)(2,1)S(1)}, u32[]{:S(2)}, u32[]{:S(2)}) collective-permute-start(bf16[30,128,128]{2,1,0:T(8,128)(2,1)} %bitcast.2), channel_id=1, source_target_pairs={{0,992},{32,0},{64,32},{96,64},{128,96},{160,128},{192,160},{224,1... | collective-permute-start | bytes 2949128 | tf_op jit(solution)/shard_map/ppermute | solution.py:18
  1.9 32.3 %collective-permute-start.1 = (bf16[20,128,128]{2,1,0:T(8,128)(2,1)}, bf16[20,128,128]{2,1,0:T(8,128)(2,1)S(1)}, u32[]{:S(2)}, u32[]{:S(2)}) collective-permute-start(bf16[20,128,128]{2,1,0:T(8,128)(2,1)} %bitcast.4), channel_id=1, source_target_pairs={{0,31},{1,0},{2,1},{3,2},{4,3},{5,4},{6,5},{7,6},{8,7},{9,8},{10,9... | collective-permute-start | bytes 1966088 | tf_op jit(solution)/shard_map/ppermute | solution.py:18
  35.5 0.0 copy-start
  35.5 1.2 copy-done
  36.7 0.0 copy-start.1
  36.7 1.1 copy-done.1
  37.8 0.0 copy-start.2
  37.8 0.7 copy-done.2
  38.4 0.0 copy-start.3
  38.4 0.7 copy-done.3
  39.1 3.6 %shard_map.64 = (f32[512,768]{1,0:T(8,128)S(1)}, s32[1,21]{1,0:T(1,128)S(1)}, s32[1,31]{1,0:T(1,128)S(1)}) custom-call(s32[1,20]{1,0:T(1,128)S(1)} %copy-done.2, s32[1,1]{1,0:T(1,128)S(6)} %copy.7.a_count, s32[1,30]{1,0:T(1,128)S(1)} %copy-done.3, s32[1,1]{1,0:T(1,128)S(6)} %copy.8.b_count, bf16[20,128,128]{2,1,0:T(8,128)(2,1)S(1)} %bitcast.5, ...), custom_call_target="tpu_custom_call" | custom-call | flops 1610612736 | bytes 8388608 | tf_op jit(solution)/shard_map/pallas_call | solution.py:72
  42.7 2.1 %collective-permute-start.2 = (s32[1,31]{1,0:T(1,128)S(1)}, s32[1,31]{1,0:T(1,128)S(1)}, u32[]{:S(2)}, u32[]{:S(2)}) collective-permute-start(s32[1,31]{1,0:T(1,128)S(1)} %get-tuple-element.9), channel_id=1, source_target_pairs={{0,992},{32,0},{64,32},{96,64},{128,96},{160,128},{192,160},{224,1... | collective-permute-start | bytes 380 | tf_op jit(solution)/shard_map/ppermute | solution.py:18
  44.8 2.6 %collective-permute-start = (s32[1,21]{1,0:T(1,128)S(1)}, s32[1,21]{1,0:T(1,128)S(1)}, u32[]{:S(2)}, u32[]{:S(2)}) collective-permute-start(s32[1,21]{1,0:T(1,128)S(1)} %get-tuple-element.8), channel_id=1, source_target_pairs={{0,31},{1,0},{2,1},{3,2},{4,3},{5,4},{6,5},{7,6},{8,7},{9,8},{10,9... | collective-permute-start | bytes 260 | tf_op jit(solution)/shard_map/ppermute | solution.py:18
  47.4 0.0 collective-permute-done.2.b_meta
  47.4 0.0 collective-permute-done.3.b_tiles
  47.4 1.3 shard_map.65.right
  48.7 105.0 %collective-permute-done.a_meta = s32[1,21]{1,0:T(1,128)S(1)} collective-permute-done((s32[1,21]{1,0:T(1,128)S(1)}, s32[1,21]{1,0:T(1,128)S(1)}, u32[]{:S(2)}, u32[]{:S(2)}) %collective-permute-start) | collective-permute-done | bytes 116 | tf_op jit(solution)/shard_map/ppermute | solution.py:18
  153.7 0.0 collective-permute-done.1.a_tiles
  153.7 3.7 %shard_map.66 = bf16[512,768]{1,0:T(8,128)(2,1)} custom-call(s32[1,21]{1,0:T(1,128)S(1)} %collective-permute-done.a_meta, bf16[20,128,128]{2,1,0:T(8,128)(2,1)S(1)} %collective-permute-done.1.a_tiles, bf16[2048,768]{1,0:T(8,128)(2,1)S(1)} %shard_map.65.right, f32[512,768]{1,0:T(8,128)S(1)} %get-tuple-element.10.total), custom_call_target="tpu_custom_call" | custom-call | flops 1610612736 | bytes 8388608 | tf_op jit(solution)/shard_map/pallas_call | solution.py:101
Async XLA Ops:
  0.0 47.4 %collective-permute-start.3 = (bf16[30,128,128]{2,1,0:T(8,128)(2,1)}, bf16[30,128,128]{2,1,0:T(8,128)(2,1)S(1)}, u32[]{:S(2)}, u32[]{:S(2)}) collective-permute-start(bf16[30,128,128]{2,1,0:T(8,128)(2,1)} %bitcast.2), channel_id=1, source_target_pairs={{0,992},{32,0},{64,32},{96,64},{128,96},{160,128},{192,160},{224,1... | collective-permute-start | bytes 2949128 | tf_op jit(solution)/shard_map/ppermute | solution.py:18
  1.9 151.8 %collective-permute-start.1 = (bf16[20,128,128]{2,1,0:T(8,128)(2,1)}, bf16[20,128,128]{2,1,0:T(8,128)(2,1)S(1)}, u32[]{:S(2)}, u32[]{:S(2)}) collective-permute-start(bf16[20,128,128]{2,1,0:T(8,128)(2,1)} %bitcast.4), channel_id=1, source_target_pairs={{0,31},{1,0},{2,1},{3,2},{4,3},{5,4},{6,5},{7,6},{8,7},{9,8},{10,9... | collective-permute-start | bytes 1966088 | tf_op jit(solution)/shard_map/ppermute | solution.py:18
  35.5 1.2 copy-start
  36.7 1.1 copy-start.1
  37.8 0.7 copy-start.2
  38.4 0.7 copy-start.3
  42.7 4.7 %collective-permute-start.2 = (s32[1,31]{1,0:T(1,128)S(1)}, s32[1,31]{1,0:T(1,128)S(1)}, u32[]{:S(2)}, u32[]{:S(2)}) collective-permute-start(s32[1,31]{1,0:T(1,128)S(1)} %get-tuple-element.9), channel_id=1, source_target_pairs={{0,992},{32,0},{64,32},{96,64},{128,96},{160,128},{192,160},{224,1... | collective-permute-start | bytes 380 | tf_op jit(solution)/shard_map/ppermute | solution.py:18
  44.8 109.0 %collective-permute-start = (s32[1,21]{1,0:T(1,128)S(1)}, s32[1,21]{1,0:T(1,128)S(1)}, u32[]{:S(2)}, u32[]{:S(2)}) collective-permute-start(s32[1,21]{1,0:T(1,128)S(1)} %get-tuple-element.8), channel_id=1, source_target_pairs={{0,31},{1,0},{2,1},{3,2},{4,3},{5,4},{6,5},{7,6},{8,7},{9,8},{10,9... | collective-permute-start | bytes 260 | tf_op jit(solution)/shard_map/ppermute | solution.py:18

commit v3 on v2

--- a/solution.py
+++ b/solution.py
@@ -49,12 +49,17 @@
     place(b_tiles, b_meta, b_meta[0, b_tiles.shape[0]], right, NT)
 
 
-def last_kernel(a_meta, a_tiles, right, total, out, left):
+def last_kernel(a_meta, a_tiles, right, total, out, left, strips, sems):
     place(a_tiles, a_meta, a_meta[0, a_tiles.shape[0]], left, KT)
-    for strip in range(0, NT * TILE, STRIP):
-        cols = pl.ds(strip, STRIP)
+    copies = []
+    for at in range(NT * TILE // STRIP):
+        cols = pl.ds(at * STRIP, STRIP)
         added = jnp.dot(left[...], right[:, cols], preferred_element_type=jnp.float32)
-        out[:, cols] = (total[:, cols] + added).astype(out.dtype)
+        strips[at] = (total[:, cols] + added).astype(out.dtype)
+        copies.append(pltpu.make_async_copy(strips.at[at], out.at[:, cols], sems.at[at]))
+        copies[-1].start()
+    for copy in copies:
+        copy.wait()
 
 
 def shards(a_tiles, a_where, a_count, b_tiles, b_where, b_count):
@@ -102,8 +107,12 @@
         last_kernel,
         out_shape=jax.ShapeDtypeStruct((rows, cols), jnp.bfloat16),
         in_specs=[smem, vmem, vmem, vmem],
-        out_specs=vmem,
-        scratch_shapes=[pltpu.VMEM((rows, depth), jnp.bfloat16)],
+        out_specs=pl.BlockSpec(memory_space=pl.ANY),
+        scratch_shapes=[
+            pltpu.VMEM((rows, depth), jnp.bfloat16),
+            pltpu.VMEM((cols // STRIP, rows, STRIP), jnp.bfloat16),
+            pltpu.SemaphoreType.DMA((cols // STRIP,)),
+        ],
         compiler_params=params,
         cost_estimate=pl.CostEstimate(flops=2 * macs, bytes_accessed=8 << 20, transcendentals=0),
     )(a_meta, a_next, right, total)

time: 158 us -> 158 us (level)
  no operation moved by 1% of the time
where the time goes in v3:
time: 158 us; the launch traced here: 157 us
  waiting for transfers between devices  106 us (67%)
  starting transfers between devices  38.8 us (25%)
  Pallas kernels  7.89 us (5%)
  local copies, waits for them, and re-layouts  3.59 us (2%)
    ppermute x4, waiting for transfers between devices, passed_along(): lax.ppermute(array, axis, [(i, (i + by) % size) for i in range(size)])  106 us
    ppermute x4, starting transfers between devices, passed_along(): lax.ppermute(array, axis, [(i, (i + by) % size) for i in range(size)])  38.8 us
    unnamed x8, local copies, waits for them, and re-layouts  3.59 us
    pallas_call x1, Pallas kernels, shards(): pl.pallas_call(last_kernel, out_shape=jax.ShapeDtypeStruct((rows, cols),...  3.47 us
    pallas_call x1, Pallas kernels, shards(): pl.pallas_call(first_kernel, out_shape=(jax.ShapeDtypeStruct((rows, cols)...  3.42 us
  transfers between devices with their start and end apart: 4, of which 1 were waited for; matrix products, arithmetic and copies ran while one was open for 0% of the time, Pallas kernels for 3%

profile of v3, /device:TPU:64, one launch (start us, length us, event | category | flops | bytes accessed | tf_op | source)
XLA Modules:
  0.0 157.2 jit_solution(10577234236171568748)
XLA Ops:
  0.0 1.9 %collective-permute-start.3 = (bf16[30,128,128]{2,1,0:T(8,128)(2,1)}, bf16[30,128,128]{2,1,0:T(8,128)(2,1)S(1)}, u32[]{:S(2)}, u32[]{:S(2)}) collective-permute-start(bf16[30,128,128]{2,1,0:T(8,128)(2,1)} %bitcast.2), channel_id=1, source_target_pairs={{0,992},{32,0},{64,32},{96,64},{128,96},{160,128},{192,160},{224,1... | collective-permute-start | bytes 2949128 | tf_op jit(solution)/shard_map/ppermute | solution.py:18
  1.9 32.3 %collective-permute-start.1 = (bf16[20,128,128]{2,1,0:T(8,128)(2,1)}, bf16[20,128,128]{2,1,0:T(8,128)(2,1)S(1)}, u32[]{:S(2)}, u32[]{:S(2)}) collective-permute-start(bf16[20,128,128]{2,1,0:T(8,128)(2,1)} %bitcast.4), channel_id=1, source_target_pairs={{0,31},{1,0},{2,1},{3,2},{4,3},{5,4},{6,5},{7,6},{8,7},{9,8},{10,9... | collective-permute-start | bytes 1966088 | tf_op jit(solution)/shard_map/ppermute | solution.py:18
  35.5 0.0 copy-start
  35.5 1.2 copy-done
  36.7 0.0 copy-start.1
  36.7 1.1 copy-done.1
  37.8 0.0 copy-start.2
  37.8 0.7 copy-done.2
  38.4 0.0 copy-start.3
  38.4 0.7 copy-done.3
  39.1 3.4 %shard_map.64 = (f32[512,768]{1,0:T(8,128)S(1)}, s32[1,21]{1,0:T(1,128)S(1)}, s32[1,31]{1,0:T(1,128)S(1)}) custom-call(s32[1,20]{1,0:T(1,128)S(1)} %copy-done.2, s32[1,1]{1,0:T(1,128)S(6)} %copy.7.a_count, s32[1,30]{1,0:T(1,128)S(1)} %copy-done.3, s32[1,1]{1,0:T(1,128)S(6)} %copy.8.b_count, bf16[20,128,128]{2,1,0:T(8,128)(2,1)S(1)} %bitcast.5, ...), custom_call_target="tpu_custom_call" | custom-call | flops 1610612736 | bytes 8388608 | tf_op jit(solution)/shard_map/pallas_call | solution.py:77
  42.5 2.6 %collective-permute-start.2 = (s32[1,31]{1,0:T(1,128)S(1)}, s32[1,31]{1,0:T(1,128)S(1)}, u32[]{:S(2)}, u32[]{:S(2)}) collective-permute-start(s32[1,31]{1,0:T(1,128)S(1)} %get-tuple-element.9), channel_id=1, source_target_pairs={{0,992},{32,0},{64,32},{96,64},{128,96},{160,128},{192,160},{224,1... | collective-permute-start | bytes 380 | tf_op jit(solution)/shard_map/ppermute | solution.py:18
  45.1 2.0 %collective-permute-start = (s32[1,21]{1,0:T(1,128)S(1)}, s32[1,21]{1,0:T(1,128)S(1)}, u32[]{:S(2)}, u32[]{:S(2)}) collective-permute-start(s32[1,21]{1,0:T(1,128)S(1)} %get-tuple-element.8), channel_id=1, source_target_pairs={{0,31},{1,0},{2,1},{3,2},{4,3},{5,4},{6,5},{7,6},{8,7},{9,8},{10,9... | collective-permute-start | bytes 260 | tf_op jit(solution)/shard_map/ppermute | solution.py:18
  47.1 0.0 collective-permute-done.2.b_meta
  47.1 0.0 collective-permute-done.3.b_tiles
  47.1 1.0 shard_map.65.right
  48.1 105.6 %collective-permute-done.a_meta = s32[1,21]{1,0:T(1,128)S(1)} collective-permute-done((s32[1,21]{1,0:T(1,128)S(1)}, s32[1,21]{1,0:T(1,128)S(1)}, u32[]{:S(2)}, u32[]{:S(2)}) %collective-permute-start) | collective-permute-done | bytes 116 | tf_op jit(solution)/shard_map/ppermute | solution.py:18
  153.7 0.0 collective-permute-done.1.a_tiles
  153.7 3.5 %shard_map.66 = bf16[512,768]{1,0:T(8,128)(2,1)} custom-call(s32[1,21]{1,0:T(1,128)S(1)} %collective-permute-done.a_meta, bf16[20,128,128]{2,1,0:T(8,128)(2,1)S(1)} %collective-permute-done.1.a_tiles, bf16[2048,768]{1,0:T(8,128)(2,1)S(1)} %shard_map.65.right, f32[512,768]{1,0:T(8,128)S(1)} %get-tuple-element.10.total), custom_call_target="tpu_custom_call" | custom-call | flops 1610612736 | bytes 8388608 | tf_op jit(solution)/shard_map/pallas_call | solution.py:106
Async XLA Ops:
  0.0 47.1 %collective-permute-start.3 = (bf16[30,128,128]{2,1,0:T(8,128)(2,1)}, bf16[30,128,128]{2,1,0:T(8,128)(2,1)S(1)}, u32[]{:S(2)}, u32[]{:S(2)}) collective-permute-start(bf16[30,128,128]{2,1,0:T(8,128)(2,1)} %bitcast.2), channel_id=1, source_target_pairs={{0,992},{32,0},{64,32},{96,64},{128,96},{160,128},{192,160},{224,1... | collective-permute-start | bytes 2949128 | tf_op jit(solution)/shard_map/ppermute | solution.py:18
  1.9 151.8 %collective-permute-start.1 = (bf16[20,128,128]{2,1,0:T(8,128)(2,1)}, bf16[20,128,128]{2,1,0:T(8,128)(2,1)S(1)}, u32[]{:S(2)}, u32[]{:S(2)}) collective-permute-start(bf16[20,128,128]{2,1,0:T(8,128)(2,1)} %bitcast.4), channel_id=1, source_target_pairs={{0,31},{1,0},{2,1},{3,2},{4,3},{5,4},{6,5},{7,6},{8,7},{9,8},{10,9... | collective-permute-start | bytes 1966088 | tf_op jit(solution)/shard_map/ppermute | solution.py:18
  35.5 1.2 copy-start
  36.7 1.1 copy-start.1
  37.8 0.7 copy-start.2
  38.4 0.7 copy-start.3
  42.5 4.6 %collective-permute-start.2 = (s32[1,31]{1,0:T(1,128)S(1)}, s32[1,31]{1,0:T(1,128)S(1)}, u32[]{:S(2)}, u32[]{:S(2)}) collective-permute-start(s32[1,31]{1,0:T(1,128)S(1)} %get-tuple-element.9), channel_id=1, source_target_pairs={{0,992},{32,0},{64,32},{96,64},{128,96},{160,128},{192,160},{224,1... | collective-permute-start | bytes 380 | tf_op jit(solution)/shard_map/ppermute | solution.py:18
  45.1 108.7 %collective-permute-start = (s32[1,21]{1,0:T(1,128)S(1)}, s32[1,21]{1,0:T(1,128)S(1)}, u32[]{:S(2)}, u32[]{:S(2)}) collective-permute-start(s32[1,21]{1,0:T(1,128)S(1)} %get-tuple-element.8), channel_id=1, source_target_pairs={{0,31},{1,0},{2,1},{3,2},{4,3},{5,4},{6,5},{7,6},{8,7},{9,8},{10,9... | collective-permute-start | bytes 260 | tf_op jit(solution)/shard_map/ppermute | solution.py:18
